TPU v7x, 32 devices: a whole 2x2x4 slice. The times are simulated.
32 devices in a mesh: row: 2 (over y), col: 16 (over z, x, core).
Axes of the slice: x: 2, y: 2, z: 4, core: 2. Of those that a mesh axis runs over, the one named last changes fastest.
Arguments:
- positions: float32 [3, 32768], P(None, ('row', 'col')), may hold values from -6 to 6
- types: int32 [32768], P(('row', 'col')), may hold values from 0 to 4
- radius_type: float32 [5], replicated, may hold values from 0.6 to 1.2
- valence_type: float32 [5], replicated, may hold values from 5 to 60
- bond_depth: float32 [5, 5], replicated, may hold values from 0.02 to 0.2
- pair_tiles: int32 [2, 16, 96, 2], P('row', 'col'), may hold values from 0 to 127, as said below
- tile_count: int32 [2, 16], P('row', 'col'), may hold values from 24 to 96, as said below
Outputs:
- force_energy: float32 [4, 32768], P(None, ('row', 'col'))
Inputs may be any that keep to these rules, and one draw needn't show every extreme that they name: `pair_tiles`: each entry is (a, b) with a below 128 and b below 16; the 96 tiles of one device are distinct. Only the first tile_count[r, c] tiles of device (r, c) are live; the most, 96, is reached on some device in every draw.
All inputs are finite; a program needn't handle non-finite values.
Results may differ from a plain program's by a relative error of at most 0.0003.
Values sent between devices are 32-bit elements; how exact they have to be, the bound alone decides.
No kernel may reach another device: no remote copies, remote signals or barrier semaphores. Data moves between devices by JAX's collectives and lax.ppermute only.
A program may use at most 64 MiB of HBM per device.

v0:
```python
import functools
import math

import jax
import jax.numpy as jnp
from jax import lax
from jax.experimental import pallas as pl
from jax.experimental.pallas import tpu as pltpu
from jax.sharding import PartitionSpec as P

TILE = 128
SUB = 8
LARGE = 64
MIDDLE = 16
SMALL = 8
LOG2E = math.log2(math.e)
SCALE = LOG2E ** (1.0 / 3.0)


def log2(size):
    return size.bit_length() - 1


def stage_bits(col_size, row_size):
    bits = [bit for bit in (col_size // 2, col_size // 4) if bit >= 2]
    return bits, col_size, row_size


def outer_part(order, col):
    total = col * 0
    for place, bit in enumerate(order[0]):
        total = total | (((col >> log2(bit)) & 1) << place)
    return total


def inner_part(order, col):
    bits, col_size, row_size = order
    return (col & ((col_size >> len(bits)) - 1)) << len(bits)


def row_part(order, row):
    return row << log2(order[1])


def col_part(order, col):
    return inner_part(order, col) | outer_part(order, col)


def pack(order, count, positions, types, tiles, packed):
    blocks_dev = types.shape[0]
    tiles_dev = tiles.shape[1]
    row = row_part(order, lax.axis_index("row"))
    col = col_part(order, lax.axis_index("col"))
    for d in range(3):
        for block in range(blocks_dev):
            place = d * blocks_dev + block
            packed[place : place + 1, :] = positions[d : d + 1, block * TILE : (block + 1) * TILE]
    packed[3 * blocks_dev : 4 * blocks_dev, :] = types[...].astype(jnp.float32)
    packed[4 * blocks_dev :, :] = jnp.zeros((SUB, TILE), jnp.float32)
    near, far = tiles[0:1, :], tiles[1:2, :]
    shift = blocks_dev.bit_length() - 1
    first = ((row | col_part(order, near >> shift)) << shift) | (near & (blocks_dev - 1))
    second = ((row_part(order, far >> shift) | col) << shift) | (far & (blocks_dev - 1))
    live = lax.broadcasted_iota(jnp.int32, (1, tiles_dev), 1) < count[0, 0]
    items = (first & 255, first >> 8, second & 255, second >> 8, jnp.where(live, 1, 0))
    for place, item in enumerate(items):
        start = 4 * blocks_dev + place
        packed[start : start + 1, 0:tiles_dev] = item.astype(jnp.float32)


def tables(elements, radius, valence, depth, rho_store, depth_store, valence_store):
    shape = (SUB, TILE)
    for t in range(elements):
        valence_store[t] = jnp.full(shape, valence[t], jnp.float32)
        for u in range(elements):
            rho = jnp.full(shape, 0.5 * (radius[t] + radius[u]), jnp.float32)
            rho_store[t * elements + u] = -SCALE / (rho * rho)
            depth_store[t * elements + u] = jnp.full(shape, depth[u, t] * (valence[u] + valence[t]), jnp.float32)


def pieces(value):
    high = value.astype(jnp.bfloat16).astype(jnp.float32)
    rest = value - high
    mid = rest.astype(jnp.bfloat16).astype(jnp.float32)
    return high, mid, rest - mid


def left_form(base, onehot):
    high, mid, low = pieces(base)
    zero = jnp.zeros_like(base)
    stack = jnp.concatenate([high, high, mid, high, low, mid, onehot, onehot, onehot, zero], axis=0)
    return stack.astype(jnp.bfloat16)


def right_geometry(base):
    high, mid, low = pieces(base)
    zero = jnp.zeros_like(base)
    stack = jnp.concatenate([high, mid, high, low, high, mid, zero, zero, zero, zero], axis=0)
    return stack.astype(jnp.bfloat16)


def right_table(rows):
    high, mid, low = pieces(rows)
    zero = jnp.zeros_like(rows)
    stack = jnp.concatenate([zero] * 6 + [high, mid, low, zero], axis=0)
    return stack.astype(jnp.bfloat16)


def force_form(base, sub_index):
    high, mid, low = pieces(base)
    rest = jnp.where(sub_index < 3, mid, jnp.where(sub_index < 6, jnp.roll(low, 3, axis=0), 0.0))
    return jnp.concatenate([high, rest], axis=0).astype(jnp.bfloat16)


def cross(left, right):
    return lax.dot_general(left, right, (((0,), (0,)), ((), ())), preferred_element_type=jnp.float32)


def fold(value):
    return jnp.sum(value.reshape(TILE // SUB, SUB, TILE), axis=0)


def kernel(
    order,
    elements,
    shift,
    rho_store,
    depth_store,
    valence,
    atoms,
    out,
    left_base,
    right_base,
    onehot,
    rho_rows,
    coord,
    right_own,
    self_weight,
    total,
    energy,
    pulls,
    ranks,
    marks,
    firsts,
    second_cols,
    own_flat,
    work_flat,
    own_list,
    work_list,
    own_sem,
    head_sem,
    work_sem,
):
    payload = 5 * SUB
    slots = atoms.shape[0] // payload
    blocks_dev = SUB
    blocks = slots * blocks_dev
    flip = outer_part(order, lax.axis_index("col")) * blocks_dev
    own_slot = row_part(order, lax.axis_index("row")) | inner_part(order, lax.axis_index("col"))
    own_base = own_slot * blocks_dev
    ones = jnp.ones((SUB, TILE), jnp.float32)
    zeros = jnp.zeros((SUB, TILE), jnp.float32)

    def put(ref, slot, row, value):
        ref[pl.ds((slot * blocks_dev + 1) * SUB + row, blocks_dev, stride=SUB), :] = value

    def prepare(slot, carry):
        start = pl.multiple_of(slot * payload, SUB)
        x = atoms[pl.ds(start, SUB), :]
        y = atoms[pl.ds(start + SUB, SUB), :]
        z = atoms[pl.ds(start + 2 * SUB, SUB), :]
        kind = atoms[pl.ds(start + 3 * SUB, SUB), :]
        square = x * x + y * y + z * z
        hot = [jnp.where(kind == float(t), 1.0, 0.0) for t in range(elements)]
        value = zeros
        for t in range(elements):
            value = value + hot[t] * valence[t]
        for row, item in enumerate((x, y, z, square, ones, value, zeros, zeros)):
            put(left_base, slot, row, item)
        for row, item in enumerate((-2.0 * x, -2.0 * y, -2.0 * z, ones, square, zeros, zeros, zeros)):
            put(right_base, slot, row, item)
        for row in range(SUB):
            put(onehot, slot, row, hot[row] if row < elements else zeros)
            if row < elements:
                mixed = hot[0] * rho_store[row * elements]
                for t in range(1, elements):
                    mixed = mixed + hot[t] * rho_store[row * elements + t]
            else:
                mixed = zeros
            put(rho_rows, slot, row, mixed)
        for block in range(blocks_dev):
            coord[slot * blocks_dev + block + 1] = zeros
        return carry

    lax.fori_loop(0, slots, prepare, 0)
    for ref in (left_base, right_base, onehot, rho_rows):
        ref[0:SUB, :] = zeros

    lane = lax.broadcasted_iota(jnp.int32, (TILE, TILE), 1)
    sublane = lax.broadcasted_iota(jnp.int32, (TILE, TILE), 0)
    before = jnp.where(sublane < lane, 1.0, 0.0).astype(jnp.bfloat16)
    slot_col = lax.broadcasted_iota(jnp.int32, (slots, slots), 1)
    slot_row = lax.broadcasted_iota(jnp.int32, (slots, slots), 0)
    above = jnp.where(slot_col < slot_row, 1.0, 0.0).astype(jnp.bfloat16)

    def meta(row):
        return atoms[pl.ds(4 * SUB + row, slots, stride=payload), :]

    first_all = (meta(0) + 256.0 * meta(1)).astype(jnp.int32) ^ flip
    live_all = meta(4)
    firsts[...] = first_all.astype(jnp.float32)

    def rank(mark):
        count = mark.astype(jnp.bfloat16)
        inside = jnp.dot(count, before, preferred_element_type=jnp.float32)
        earlier = jnp.dot(above, count, preferred_element_type=jnp.float32)
        place = inside + jnp.sum(earlier, axis=1, keepdims=True)
        ranks[...] = jnp.where(mark > 0.0, place, -1.0)
        return jnp.sum(mark).astype(jnp.int32)

    position = sublane.astype(jnp.float32)
    batch = min(slots, 4 * SUB)

    def compact(chunk, flat, columns):
        offset = jnp.float32(1.0) * (chunk * TILE)

        def some(group, carry):
            total = carry
            for part in range(batch // SUB):
                start = pl.multiple_of(group * batch + part * SUB, SUB)
                wanted = ranks[pl.ds(start, SUB), :] - offset
                picks = [
                    jnp.where(wanted[k : k + 1] == position, 1.0, 0.0).astype(jnp.bfloat16) for k in range(SUB)
                ]
                entries = [
                    atoms[pl.ds(pl.multiple_of((start + k) * payload + 4 * SUB, SUB), SUB), :].astype(
                        jnp.bfloat16
                    )
                    for k in range(SUB)
                ]
                total = total + lax.dot_general(
                    jnp.concatenate(entries, axis=1),
                    jnp.concatenate(picks, axis=1),
                    (((1,), (1,)), ((), ())),
                    preferred_element_type=jnp.float32,
                )
            return total

        row = lax.fori_loop(0, slots // batch, some, zeros)
        first = (row[0:1] + 256.0 * row[1:2]).astype(jnp.int32) ^ flip
        second = (row[2:3] + 256.0 * row[3:4]).astype(jnp.int32) ^ flip
        valid = row[4:5] > 0.0
        flat[pl.ds(chunk, 1), :] = jnp.where(valid, ((first + 1) << shift) | (second + 1), 0)
        if columns:
            target = jnp.where(valid, second, -1).astype(jnp.float32)
            column = jnp.transpose(jnp.broadcast_to(target, (SUB, TILE)))[:, 0:1]
            second_cols[...] = jnp.broadcast_to(column, (TILE, TILE))

    def send(source, target, group, semaphore):
        start = pl.multiple_of(group * SUB, SUB)
        return pltpu.make_async_copy(source.at[pl.ds(start, SUB)], target.at[pl.ds(start, SUB)], semaphore)

    def send_rest(source, target, count, semaphore):
        def one(group, carry):
            copy = send(source, target, group, semaphore)
            copy.start()
            copy.wait()
            return carry

        lax.fori_loop(1, (count + SUB * TILE - 1) // (SUB * TILE), one, 0)

    own_mark = jnp.where((first_all >> log2(blocks_dev)) == own_slot, live_all, 0.0)
    marks[...] = own_mark
    own_count = rank(own_mark)

    def own_chunk(chunk, carry):
        compact(chunk, own_flat, True)
        part = 4 * SUB
        filled = jnp.minimum(own_count - chunk * TILE, TILE)

        def some(group, carry):
            cols = second_cols[pl.ds(pl.multiple_of(group * part, part), part), :]

            def rows(slot_group, carry):
                for piece in range(batch // SUB):
                    start = pl.multiple_of(slot_group * batch + piece * SUB, SUB)
                    here = firsts[pl.ds(start, SUB), :]
                    found = []
                    for k in range(SUB):
                        hit = jnp.where(cols == here[k : k + 1], 1.0, 0.0)
                        found.append(jnp.max(hit, axis=0, keepdims=True))
                    old = marks[pl.ds(start, SUB), :]
                    marks[pl.ds(start, SUB), :] = jnp.maximum(old, jnp.concatenate(found, axis=0))
                return carry

            return lax.fori_loop(0, slots // batch, rows, carry)

        lax.fori_loop(0, (filled + part - 1) // part, some, 0)
        return carry

    lax.fori_loop(0, (own_count + TILE - 1) // TILE, own_chunk, 0)
    send_rest(own_flat, own_list, own_count, own_sem)
    own_copy = send(own_flat, own_list, 0, own_sem)
    own_copy.start()

    work_count = rank(marks[...] * live_all)

    head_copy = pltpu.make_async_copy(work_flat.at[pl.ds(0, 1)], work_list.at[pl.ds(0, 1)], head_sem)
    compact(0, work_flat, False)
    head_copy.start()

    def work_chunk(chunk, carry):
        compact(chunk, work_flat, False)
        return carry

    lax.fori_loop(1, (work_count + TILE - 1) // TILE, work_chunk, 0)
    send_rest(work_flat, work_list, work_count, work_sem)
    rest_copy = pltpu.make_async_copy(
        work_flat.at[pl.ds(1, SUB - 1)], work_list.at[pl.ds(1, SUB - 1)], work_sem
    )
    rest_copy.start()
    head_copy.wait()
    own_copy.wait()

    def at(ref, block):
        return ref[pl.ds(pl.multiple_of(block * SUB, SUB), SUB), :]

    def fetch(ref, start):
        row = lax.shift_right_logical(start, TILE.bit_length() - 1)
        column = start & (TILE - 1)

        def at_step(step):
            code = ref[row, column + step]
            return code >> shift, code & ((1 << shift) - 1)

        return at_step

    def first_pass(start, size):
        pair = fetch(work_list, start)
        for step in range(size):
            first, second = pair(step)
            left = left_form(at(left_base, second), at(onehot, second))
            right = jnp.concatenate(
                [right_geometry(at(right_base, first)), right_table(at(rho_rows, first))], axis=1
            )
            both = cross(left, right)
            ratio = both[:, :TILE] * both[:, TILE:]
            bond = jnp.exp2(ratio * ratio * ratio)
            same = jnp.where(first == second, 1.0 / SUB, 0.0)
            coord[first] = coord[first] + (fold(bond) - same)

    fulls = work_count // LARGE
    early = TILE // LARGE

    def large(group, carry):
        first_pass(group * LARGE, LARGE)
        return carry

    def small(group, carry):
        first_pass(group * SMALL, SMALL)
        return carry

    lax.fori_loop(0, jnp.minimum(fulls, early), large, 0)
    rest_copy.wait()
    lax.fori_loop(jnp.minimum(fulls, early), fulls, large, 0)

    def middle(group, carry):
        first_pass(group * MIDDLE, MIDDLE)
        return carry

    edge = (work_count + MIDDLE - SMALL - 1) // MIDDLE
    lax.fori_loop(fulls * (LARGE // MIDDLE), edge, middle, 0)
    lax.fori_loop(edge * (MIDDLE // SMALL), (work_count + SMALL - 1) // SMALL, small, 0)

    sub_index = lax.broadcasted_iota(jnp.int32, (SUB, TILE), 0)

    for block in range(blocks_dev):
        place = own_base + block + 1
        base = at(left_base, place)
        hot = at(onehot, place)
        load = jnp.sum(coord[place], axis=0, keepdims=True) + base[5:6]
        depth_rows = zeros
        for row in range(elements):
            mixed = hot[0:1] * depth_store[row * elements, 0:1]
            for t in range(1, elements):
                mixed = mixed + hot[t : t + 1] * depth_store[row * elements + t, 0:1]
            depth_rows = jnp.where(sub_index == row, mixed, depth_rows)
        load_rows = jnp.where(sub_index == 4, load, jnp.where(sub_index == 5, 1.0, 0.0))
        forms = [
            right_geometry(at(right_base, place)),
            right_table(at(rho_rows, place)),
            right_table(depth_rows),
            right_geometry(load_rows),
        ]
        alone = hot[0:1] * depth_store[0, 0:1]
        for t in range(1, elements):
            alone = alone + hot[t : t + 1] * depth_store[t * elements + t, 0:1]
        self_weight[block + 1] = jnp.where(sub_index == 0, alone / (load + load), 0.0)
        right_own[block + 1] = jnp.concatenate(forms, axis=1)
    self_weight[0] = zeros
    right_own[0] = jnp.zeros(right_own.shape[1:], jnp.bfloat16)
    for block in range(blocks_dev + 1):
        total[block] = jnp.zeros(total.shape[1:], jnp.float32)
        energy[block] = zeros

    def second_pass(start, size):
        pair = fetch(own_list, start)
        for step in range(size):
            first, second = pair(step)
            load = jnp.sum(coord[second], axis=0, keepdims=True)
            base = at(left_base, second)
            base = base + jnp.where(sub_index == 5, load, 0.0)
            left = left_form(base, at(onehot, second))
            local_first = jnp.maximum(first - own_base, 0)
            mixed = cross(left, right_own[local_first])
            dist, rho, depth, both_load = [mixed[:, k * TILE : (k + 1) * TILE] for k in range(4)]
            ratio = dist * rho
            squared = ratio * ratio
            bond = jnp.exp2(squared * ratio)
            weight = depth * bond / both_load
            pull = weight * squared * rho
            pull_high = pull.astype(jnp.bfloat16)
            pulls[step, :, 0:TILE] = pull_high
            pulls[step, :, TILE:] = (pull - pull_high.astype(jnp.float32)).astype(jnp.bfloat16)
            same = jnp.where(first == second, 1.0, 0.0)
            update = fold(weight) - same * self_weight[local_first]
            energy[local_first] = energy[local_first] + update
        for step in range(size):
            first, second = pair(step)
            form = force_form(at(left_base, second), sub_index)
            sums = jnp.dot(form, pulls[step], preferred_element_type=jnp.float32)
            local_first = jnp.maximum(first - own_base, 0)
            total[local_first] = total[local_first] + sums

    def second_group(group, carry):
        second_pass(group * SMALL, SMALL)
        return carry

    def second_large(group, carry):
        second_pass(group * MIDDLE, MIDDLE)
        return carry

    middles = (own_count + MIDDLE - SMALL - 1) // MIDDLE
    lax.fori_loop(0, middles, second_large, 0)
    lax.fori_loop(middles * (MIDDLE // SMALL), (own_count + SMALL - 1) // SMALL, second_group, 0)

    for block in range(blocks_dev):
        both = total[block + 1]
        sums = both[:, :TILE] + both[:, TILE:]
        here = at(left_base, own_base + block + 1)
        lanes = slice(block * TILE, (block + 1) * TILE)
        for d in range(3):
            moment = sums[d : d + 1] + sums[8 + d : 9 + d] + sums[11 + d : 12 + d]
            out[d : d + 1, lanes] = (-6.0 / LOG2E) * (moment - here[d : d + 1] * sums[4:5])
        out[3:4, lanes] = -jnp.sum(energy[block + 1], axis=0, keepdims=True)


def local(order, positions, types, radius_type, valence_type, bond_depth, pair_tiles, tile_count):
    atom_dev = positions.shape[1]
    blocks_dev = atom_dev // TILE
    rows = lax.axis_size("row")
    cols = lax.axis_size("col")
    slots = rows * cols
    blocks = slots * blocks_dev
    tiles_dev = pair_tiles.shape[2]

    smem = pl.BlockSpec(memory_space=pltpu.SMEM)
    vmem = pl.BlockSpec(memory_space=pltpu.VMEM)
    packed = pl.pallas_call(
        functools.partial(pack, order),
        out_shape=pltpu.VMEM((5 * SUB, TILE), jnp.float32),
        in_specs=[smem, vmem, vmem, vmem],
        out_specs=vmem,
    )(tile_count, positions, types.reshape(blocks_dev, TILE), jnp.transpose(pair_tiles[0, 0]))
    elements = radius_type.shape[0]
    squares = (elements * elements, SUB, TILE)
    stores = pl.pallas_call(
        functools.partial(tables, elements),
        out_shape=(
            pltpu.VMEM(squares, jnp.float32),
            pltpu.VMEM(squares, jnp.float32),
            pltpu.VMEM((elements, SUB, TILE), jnp.float32),
        ),
        in_specs=[smem, smem, smem],
        out_specs=(vmem, vmem, vmem),
    )(radius_type, valence_type, bond_depth)

    gathered = packed
    for bit in order[0]:
        other = lax.ppermute(gathered, "col", [(i, i ^ bit) for i in range(cols)])
        gathered = jnp.concatenate([gathered, other], axis=0)
    inner = cols >> len(order[0])
    groups = [
        [row * cols + start + k for row in range(rows) for k in range(inner)] for start in range(0, cols, inner)
    ]
    gathered = lax.all_gather(gathered, ("row", "col"), axis=0, axis_index_groups=groups, tiled=True)

    gathered = pltpu.with_memory_space_constraint(gathered, pltpu.VMEM)
    stores = [pltpu.with_memory_space_constraint(store, pltpu.VMEM) for store in stores]
    shift = (blocks + 1).bit_length()
    chunks = -(-slots * tiles_dev // (SUB * TILE)) * SUB
    own_chunks = -(-cols * tiles_dev // (SUB * TILE)) * SUB
    return pl.pallas_call(
        functools.partial(kernel, order, elements, shift),
        out_shape=jax.ShapeDtypeStruct((4, atom_dev), jnp.float32),
        in_specs=[vmem, vmem, vmem, vmem],
        out_specs=vmem,
        scratch_shapes=[
            pltpu.VMEM((blocks * SUB + SUB, TILE), jnp.float32),
            pltpu.VMEM((blocks * SUB + SUB, TILE), jnp.float32),
            pltpu.VMEM((blocks * SUB + SUB, TILE), jnp.float32),
            pltpu.VMEM((blocks * SUB + SUB, TILE), jnp.float32),
            pltpu.VMEM((blocks + 1, SUB, TILE), jnp.float32),
            pltpu.VMEM((blocks_dev + 1, 10 * SUB, 4 * TILE), jnp.bfloat16),
            pltpu.VMEM((blocks_dev + 1, SUB, TILE), jnp.float32),
            pltpu.VMEM((blocks_dev + 1, 2 * SUB, 2 * TILE), jnp.float32),
            pltpu.VMEM((blocks_dev + 1, SUB, TILE), jnp.float32),
            pltpu.VMEM((MIDDLE, TILE, 2 * TILE), jnp.bfloat16),
            pltpu.VMEM((slots, TILE), jnp.float32),
            pltpu.VMEM((slots, TILE), jnp.float32),
            pltpu.VMEM((slots, TILE), jnp.float32),
            pltpu.VMEM((TILE, TILE), jnp.float32),
            pltpu.VMEM((own_chunks, TILE), jnp.int32),
            pltpu.VMEM((chunks, TILE), jnp.int32),
            pltpu.SMEM((own_chunks, TILE), jnp.int32),
            pltpu.SMEM((chunks, TILE), jnp.int32),
            pltpu.SemaphoreType.DMA,
            pltpu.SemaphoreType.DMA,
            pltpu.SemaphoreType.DMA,
        ],
        compiler_params=pltpu.CompilerParams(vmem_limit_bytes=56 * 1024 * 1024),
    )(*stores, gathered)


def solution(mesh):
    order = stage_bits(mesh.shape["col"], mesh.shape["row"])
    in_specs = (
        P(None, ("row", "col")),
        P(("row", "col")),
        P(),
        P(),
        P(),
        P("row", "col", None, None),
        P("row", "col"),
    )
    out_specs = P(None, ("row", "col"))
    return jax.shard_map(
        functools.partial(local, order), mesh=mesh, in_specs=in_specs, out_specs=out_specs, check_vma=False
    )
```

profile of v0, /device:TPU:1, one launch (start us, length us, event | category | flops | bytes accessed | tf_op | source)
XLA Modules:
  0.0 33.6 jit_solution(6962433832838300496)
XLA Ops:
  0.7 0.8 %shard_map.74 = f32[40,128]{1,0:T(8,128)S(1)} custom-call(s32[1,1]{1,0:T(1,128)S(6)} %copy.8.count, f32[3,1024]{1,0:T(4,128)} %positions.1, s32[8,128]{1,0:T(8,128)} %bitcast.4, s32[2,96]{1,0:T(2,128)} %bitcast.5), custom_call_target="tpu_custom_call" | custom-call | tf_op jit(solution)/shard_map/pallas_call | solution.py:469
  1.4 3.2 %collective-permute-start = (f32[40,128]{1,0:T(8,128)S(1)}, f32[40,128]{1,0:T(8,128)S(1)}, u32[]{:S(2)}, u32[]{:S(2)}) collective-permute-start(f32[40,128]{1,0:T(8,128)S(1)} %shard_map.74), channel_id=1, source_target_pairs={{0,8},{1,9},{2,10},{3,11},{4,12},{5,13},{6,14},{7,15},{8,0},{9,1},... | collective-permute-start | bytes 61448 | tf_op jit(solution)/shard_map/ppermute | solution.py:490
  4.6 1.2 %collective-permute-done = f32[40,128]{1,0:T(8,128)S(1)} collective-permute-done((f32[40,128]{1,0:T(8,128)S(1)}, f32[40,128]{1,0:T(8,128)S(1)}, u32[]{:S(2)}, u32[]{:S(2)}) %collective-permute-start) | collective-permute-done | bytes 20512 | tf_op jit(solution)/shard_map/ppermute | solution.py:490
  5.8 1.4 %collective-permute-start.1 = (f32[80,128]{1,0:T(8,128)S(1)}, f32[80,128]{1,0:T(8,128)S(1)}, u32[]{:S(2)}, u32[]{:S(2)}) collective-permute-start(f32[80,128]{1,0:T(8,128)S(1)} %pad_maximum_fusion.1), channel_id=1, source_target_pairs={{0,4},{1,5},{2,6},{3,7},{4,0},{5,1},{6,2},{7,3},{8,12},{9,13},{10,... | collective-permute-start | bytes 122888 | tf_op jit(solution)/shard_map/ppermute | solution.py:490
  7.2 0.8 %shard_map.73 = (f32[25,8,128]{2,1,0:T(8,128)S(1)}, f32[25,8,128]{2,1,0:T(8,128)S(1)}, f32[5,8,128]{2,1,0:T(8,128)S(1)}) custom-call(f32[5]{0:T(128)} %radius.1, f32[5]{0:T(128)} %valence.1, f32[5,5]{1,0:T(8,128)} %depth.1), custom_call_target="tpu_custom_call" | custom-call | tf_op jit(solution)/shard_map/pallas_call | solution.py:477
  7.9 0.7 %collective-permute-done.1 = f32[80,128]{1,0:T(8,128)S(1)} collective-permute-done((f32[80,128]{1,0:T(8,128)S(1)}, f32[80,128]{1,0:T(8,128)S(1)}, u32[]{:S(2)}, u32[]{:S(2)}) %collective-permute-start.1) | collective-permute-done | bytes 40992 | tf_op jit(solution)/shard_map/ppermute | solution.py:490
  8.7 13.1 %all_gather.3.atoms = f32[1280,128]{1,0:T(8,128)S(1)} all-gather(f32[160,128]{1,0:T(8,128)S(1)} %pad_maximum_fusion), channel_id=1, replica_groups={{0,1,2,3,16,17,18,19},{4,5,6,7,20,21,22,23},{8,9,10,11,24,25,26,27},{12..., dimensions={0}, use_global_device_ids=true | all-gather | bytes 737280 | tf_op jit(solution)/shard_map/all_gather | solution.py:496
  21.7 11.9 %shard_map.75 = f32[4,1024]{1,0:T(4,128)} custom-call(f32[25,8,128]{2,1,0:T(8,128)S(1)} %get-tuple-element.8.rho_store, f32[25,8,128]{2,1,0:T(8,128)S(1)} %get-tuple-element.9.depth_store, f32[5,8,128]{2,1,0:T(8,128)S(1)} %get-tuple-element.10.valence, f32[1280,128]{1,0:T(8,128)S(1)} %all_gather.3.atoms), custom_call_target="tpu_custom_call" | custom-call | tf_op jit(solution)/shard_map/pallas_call | solution.py:503
  (2 shorter events, 0.0 us)
Async XLA Ops:
  1.4 4.4 %collective-permute-start = (f32[40,128]{1,0:T(8,128)S(1)}, f32[40,128]{1,0:T(8,128)S(1)}, u32[]{:S(2)}, u32[]{:S(2)}) collective-permute-start(f32[40,128]{1,0:T(8,128)S(1)} %shard_map.74), channel_id=1, source_target_pairs={{0,8},{1,9},{2,10},{3,11},{4,12},{5,13},{6,14},{7,15},{8,0},{9,1},... | collective-permute-start | bytes 61448 | tf_op jit(solution)/shard_map/ppermute | solution.py:490
  5.8 2.9 %collective-permute-start.1 = (f32[80,128]{1,0:T(8,128)S(1)}, f32[80,128]{1,0:T(8,128)S(1)}, u32[]{:S(2)}, u32[]{:S(2)}) collective-permute-start(f32[80,128]{1,0:T(8,128)S(1)} %pad_maximum_fusion.1), channel_id=1, source_target_pairs={{0,4},{1,5},{2,6},{3,7},{4,0},{5,1},{6,2},{7,3},{8,12},{9,13},{10,... | collective-permute-start | bytes 122888 | tf_op jit(solution)/shard_map/ppermute | solution.py:490
where the time goes:
time: 33.8 us; the launch traced here: 33.6 us
  Pallas kernels  13.4 us (40%)
  blocking collectives  13.1 us (39%)
  starting transfers between devices  4.56 us (13%)
  waiting for transfers between devices  1.88 us (6%)
  between operations  0.66 us (2%)
    all_gather x1, blocking collectives, local(): lax.all_gather(gathered, ('row', 'col'), axis=0, axis_index_groups=groups...  13.1 us
    pallas_call x1, Pallas kernels, local(): pl.pallas_call(functools.partial(kernel, order, elements, shift), out_sha...  11.9 us
    ppermute x2, starting transfers between devices, local(): other = lax.ppermute(gathered, 'col', [(i, i ^ bit) for i in range(cols)])  4.56 us
    ppermute x2, waiting for transfers between devices, local(): other = lax.ppermute(gathered, 'col', [(i, i ^ bit) for i in range(cols)])  1.88 us
    pallas_call x1, Pallas kernels, local(): pl.pallas_call(functools.partial(tables, elements), out_shape=(pltpu.VMEM...  0.78 us
    pallas_call x1, Pallas kernels, local(): pl.pallas_call(functools.partial(pack, order), out_shape=pltpu.VMEM((5 *...  0.76 us
  transfers between devices with their start and end apart: 2, of which 2 were waited for; matrix products, arithmetic and copies ran while one was open for 0% of the time, Pallas kernels for 2%

commit v1 on v0

--- a/solution.py
+++ b/solution.py
@@ -11,7 +11,7 @@
 TILE = 128
 SUB = 8
 LARGE = 64
-MIDDLE = 16
+MIDDLE = 32
 SMALL = 8
 LOG2E = math.log2(math.e)
 SCALE = LOG2E ** (1.0 / 3.0)

time: 33.8 us -> 34.7 us (1.027)
  the two profiles are of different devices: /device:TPU:1 before, /device:TPU:13 now
where the time goes in v1:
time: 34.7 us; the launch traced here: 34.9 us
  Pallas kernels  15.7 us (45%)
  blocking collectives  12.9 us (37%)
  waiting for transfers between devices  3.13 us (9%)
  starting transfers between devices  2.54 us (7%)
  between operations  0.66 us (2%)
    pallas_call x1, Pallas kernels, local(): pl.pallas_call(functools.partial(kernel, order, elements, shift), out_sha...  14.1 us
    all_gather x1, blocking collectives, local(): lax.all_gather(gathered, ('row', 'col'), axis=0, axis_index_groups=groups...  12.9 us
    ppermute x2, waiting for transfers between devices, local(): other = lax.ppermute(gathered, 'col', [(i, i ^ bit) for i in range(cols)])  3.13 us
    ppermute x2, starting transfers between devices, local(): other = lax.ppermute(gathered, 'col', [(i, i ^ bit) for i in range(cols)])  2.54 us
    pallas_call x1, Pallas kernels, local(): pl.pallas_call(functools.partial(tables, elements), out_shape=(pltpu.VMEM...  0.78 us
    pallas_call x1, Pallas kernels, local(): pl.pallas_call(functools.partial(pack, order), out_shape=pltpu.VMEM((5 *...  0.76 us
  transfers between devices with their start and end apart: 2, of which 2 were waited for; matrix products, arithmetic and copies ran while one was open for 0% of the time, Pallas kernels for 2%

profile of v1, /device:TPU:13, one launch (start us, length us, event | category | flops | bytes accessed | tf_op | source)
XLA Modules:
  0.0 34.9 jit_solution(18209255075309013031)
XLA Ops:
  0.7 0.8 %shard_map.74 = f32[40,128]{1,0:T(8,128)S(1)} custom-call(s32[1,1]{1,0:T(1,128)S(6)} %copy.8.count, f32[3,1024]{1,0:T(4,128)} %positions.1, s32[8,128]{1,0:T(8,128)} %bitcast.4, s32[2,96]{1,0:T(2,128)} %bitcast.5), custom_call_target="tpu_custom_call" | custom-call | tf_op jit(solution)/shard_map/pallas_call | solution.py:469
  1.4 2.4 %collective-permute-start = (f32[40,128]{1,0:T(8,128)S(1)}, f32[40,128]{1,0:T(8,128)S(1)}, u32[]{:S(2)}, u32[]{:S(2)}) collective-permute-start(f32[40,128]{1,0:T(8,128)S(1)} %shard_map.74), channel_id=1, source_target_pairs={{0,8},{1,9},{2,10},{3,11},{4,12},{5,13},{6,14},{7,15},{8,0},{9,1},... | collective-permute-start | bytes 61448 | tf_op jit(solution)/shard_map/ppermute | solution.py:490
  3.8 1.2 %collective-permute-done = f32[40,128]{1,0:T(8,128)S(1)} collective-permute-done((f32[40,128]{1,0:T(8,128)S(1)}, f32[40,128]{1,0:T(8,128)S(1)}, u32[]{:S(2)}, u32[]{:S(2)}) %collective-permute-start) | collective-permute-done | bytes 20512 | tf_op jit(solution)/shard_map/ppermute | solution.py:490
  5.0 0.2 collective-permute-start.1
  5.2 0.8 %shard_map.73 = (f32[25,8,128]{2,1,0:T(8,128)S(1)}, f32[25,8,128]{2,1,0:T(8,128)S(1)}, f32[5,8,128]{2,1,0:T(8,128)S(1)}) custom-call(f32[5]{0:T(128)} %radius.1, f32[5]{0:T(128)} %valence.1, f32[5,5]{1,0:T(8,128)} %depth.1), custom_call_target="tpu_custom_call" | custom-call | tf_op jit(solution)/shard_map/pallas_call | solution.py:477
  6.0 1.9 %collective-permute-done.1 = f32[80,128]{1,0:T(8,128)S(1)} collective-permute-done((f32[80,128]{1,0:T(8,128)S(1)}, f32[80,128]{1,0:T(8,128)S(1)}, u32[]{:S(2)}, u32[]{:S(2)}) %collective-permute-start.1) | collective-permute-done | bytes 40992 | tf_op jit(solution)/shard_map/ppermute | solution.py:490
  7.9 12.9 %all_gather.3.atoms = f32[1280,128]{1,0:T(8,128)S(1)} all-gather(f32[160,128]{1,0:T(8,128)S(1)} %pad_maximum_fusion), channel_id=1, replica_groups={{0,1,2,3,16,17,18,19},{4,5,6,7,20,21,22,23},{8,9,10,11,24,25,26,27},{12..., dimensions={0}, use_global_device_ids=true | all-gather | bytes 737280 | tf_op jit(solution)/shard_map/all_gather | solution.py:496
  20.8 14.1 %shard_map.75 = f32[4,1024]{1,0:T(4,128)} custom-call(f32[25,8,128]{2,1,0:T(8,128)S(1)} %get-tuple-element.8.rho_store, f32[25,8,128]{2,1,0:T(8,128)S(1)} %get-tuple-element.9.depth_store, f32[5,8,128]{2,1,0:T(8,128)S(1)} %get-tuple-element.10.valence, f32[1280,128]{1,0:T(8,128)S(1)} %all_gather.3.atoms), custom_call_target="tpu_custom_call" | custom-call | tf_op jit(solution)/shard_map/pallas_call | solution.py:503
  (2 shorter events, 0.0 us)
Async XLA Ops:
  1.4 3.6 %collective-permute-start = (f32[40,128]{1,0:T(8,128)S(1)}, f32[40,128]{1,0:T(8,128)S(1)}, u32[]{:S(2)}, u32[]{:S(2)}) collective-permute-start(f32[40,128]{1,0:T(8,128)S(1)} %shard_map.74), channel_id=1, source_target_pairs={{0,8},{1,9},{2,10},{3,11},{4,12},{5,13},{6,14},{7,15},{8,0},{9,1},... | collective-permute-start | bytes 61448 | tf_op jit(solution)/shard_map/ppermute | solution.py:490
  5.0 2.9 %collective-permute-start.1 = (f32[80,128]{1,0:T(8,128)S(1)}, f32[80,128]{1,0:T(8,128)S(1)}, u32[]{:S(2)}, u32[]{:S(2)}) collective-permute-start(f32[80,128]{1,0:T(8,128)S(1)} %pad_maximum_fusion.1), channel_id=1, source_target_pairs={{0,4},{1,5},{2,6},{3,7},{4,0},{5,1},{6,2},{7,3},{8,12},{9,13},{10,... | collective-permute-start | bytes 122888 | tf_op jit(solution)/shard_map/ppermute | solution.py:490
